TPU v7x, 256 devices: a whole 4x4x8 slice. The times are simulated.
256 devices in a mesh: tok: 32 (over x, z_hi, core), hid: 8 (over y, z_lo).
Axes of the slice: x: 4, y: 4, z: 8 (z_hi: 4, z_lo: 2; z = z_hi * 2 + z_lo), core: 2. Of those that a mesh axis runs over, the one named last changes fastest.
Arguments:
- base: float32 [1024, 16384], P('tok', 'hid'), may hold values from -6 to 6
- source: float32 [1024, 16384], P('tok', 'hid'), may hold values from -6 to 6
- pairs: int32 [1024], replicated, may hold values from 0 to 1023, each once
- counts: int32 [1024], replicated, may hold values from 1 to 128
- rotation: float32 [16384, 16384], P('hid', 'tok'), may hold values from -0.046875 to 0.046875
Outputs:
- patched: float32 [1024, 16384], P('tok', 'hid')
All inputs are finite; a program needn't handle non-finite values.
Results may differ from a plain program's by a relative error of at most 0.000075.
Values sent between devices are 32-bit elements; how exact they have to be, the bound alone decides.
No kernel may reach another device: no remote copies, remote signals or barrier semaphores. Data moves between devices by JAX's collectives and lax.ppermute only.
A program may use at most 64 MiB of HBM per device.

v0:
```python
import jax
import jax.numpy as jnp
from jax import lax
from jax.sharding import PartitionSpec as P

BLOCK = 128


def local(base, source, pairs, counts, rotation):
    high = lax.Precision.HIGH
    stacked = jnp.stack([base, source])
    terms = jnp.einsum(
        "srk,kc->src",
        lax.all_gather(stacked, "tok", axis=1, tiled=True),
        rotation,
        precision=high,
        preferred_element_type=jnp.float32,
    )
    width = rotation.shape[1]
    columns = lax.axis_index("tok") * width + jnp.arange(width, dtype=jnp.int32)
    source_terms = terms[1].at[pairs].get(mode="promise_in_bounds")
    chosen = columns[None, :] < (counts * BLOCK)[:, None]
    mixed_terms = jnp.where(chosen, source_terms, terms[0])
    mixed = lax.psum_scatter(mixed_terms, "hid", scatter_dimension=0, tiled=True)
    full = lax.all_gather(mixed, "hid", axis=0, tiled=True)
    return lax.psum_scatter(
        lax.dot_general(
            full,
            rotation,
            (((1,), (1,)), ((), ())),
            precision=high,
            preferred_element_type=jnp.float32,
        ),
        "tok",
        scatter_dimension=0,
        tiled=True,
    )


def solution(mesh):
    return jax.shard_map(
        local,
        mesh=mesh,
        in_specs=(P("tok", "hid"), P("tok", "hid"), P(), P(), P("hid", "tok")),
        out_specs=P("tok", "hid"),
        check_vma=False,
    )
```

profile of v0, /device:TPU:8, one launch (start us, length us, event | category | flops | bytes accessed | tf_op | source)
XLA Modules:
  0.0 408.1 jit_solution(10184686571337439872)
XLA Ops:
  6.5 0.0 all-gather.3.cloned.1.call-start
  6.5 1.9 pad_maximum_fusion
  8.4 0.0 all-gather.3.cloned.1.call-update
  8.4 0.0 reduce-scatter.3.cloned.1.call-start
  8.5 0.7 fusion.3
  9.2 0.7 broadcast_multiply_fusion
  9.9 107.8 %all-gather.3.cloned.1.call-done = f32[2,1024,2048]{2,1,0:T(8,128)} async-done(((f32[2,32,2048]{2,1,0:T(8,128)}), f32[2,1024,2048]{2,1,0:T(8,128)}) %all-gather.3.cloned.1.call-update) | async-done | bytes 16777232 | tf_op jit(solution)/shard_map/all_gather | solution.py:14
  117.7 17.7 %fusion = f32[2,1024,512]{2,1,0:T(8,128)S(1)} fusion(f32[2,1024,2048]{2,1,0:T(8,128)} %all-gather.3.cloned.1.call-done, f32[2048,512]{1,0:T(8,128)} %param.9), kind=kOutput, calls=%fused_computation.1 | convolution fusion | flops 12884901888 | bytes 25165824 | tf_op jit(solution)/shard_map/srk,kc->src/dot_general | solution.py:12
  135.4 0.0 copy-start
  135.4 1.9 copy-done
  137.4 0.2 slice_bitcast_fusion.1
  137.5 4.9 %gather_fusion = f32[1024,512]{1,0:T(8,128)} fusion(f32[1024,512]{1,0:T(8,128)S(1)} %slice_bitcast_fusion.1, s32[1024]{0:T(1024)S(1)} %fusion.3), kind=kCustom, calls=%fused_computation | custom fusion | bytes 4198400 | tf_op jit(solution)/shard_map/gather | solution.py:21
  142.4 3.8 fusion.2
  146.2 0.0 reduce-scatter.3.cloned.1.call-update
  146.3 0.0 all-gather.5.cloned.1.call-start
  146.3 65.4 %reduce-scatter.3.cloned.1.call-done = f32[128,512]{1,0:T(8,128)} async-done(((f32[1024,512]{1,0:T(8,128)}), f32[128,512]{1,0:T(8,128)}) %reduce-scatter.3.cloned.1.call-update) | async-done | bytes 262160 | tf_op jit(solution)/shard_map/reduce_scatter | solution.py:24
  211.7 0.0 all-gather.5.cloned.1.call-update
  211.7 0.0 reduce-scatter.5.cloned.1.call-start
  211.8 55.7 %all-gather.5.cloned.1.call-done = f32[1024,512]{1,0:T(8,128)} async-done(((f32[128,512]{1,0:T(8,128)}), f32[1024,512]{1,0:T(8,128)}) %all-gather.5.cloned.1.call-update) | async-done | bytes 2097168 | tf_op jit(solution)/shard_map/all_gather | solution.py:25
  267.5 11.6 %fusion.4 = f32[1024,2048]{1,0:T(8,128)} fusion(f32[1024,512]{1,0:T(8,128)} %all-gather.5.cloned.1.call-done, f32[2048,512]{1,0:T(8,128)} %param.9), kind=kOutput, calls=%fused_computation.11 | convolution fusion | flops 6442450944 | bytes 14680064 | tf_op jit(solution)/shard_map/dot_general | solution.py:27
  279.1 0.0 reduce-scatter.5.cloned.1.call-update
  279.1 122.5 %reduce-scatter.5.cloned.1.call-done = f32[32,2048]{1,0:T(8,128)} async-done(((f32[1024,2048]{1,0:T(8,128)}), f32[32,2048]{1,0:T(8,128)}) %reduce-scatter.5.cloned.1.call-update) | async-done | bytes 262160 | tf_op jit(solution)/shard_map/reduce_scatter | solution.py:26
  (1 shorter events, 0.0 us)
Async XLA Ops:
  6.5 111.2 %all-gather.3.cloned.1.call-start = ((), (), s32[]{:S(2)}) async-start(), calls=%async_computation.2 | async-start | bytes 17301504 | tf_op jit(solution)/shard_map/all_gather | solution.py:14
  8.4 203.3 %reduce-scatter.3.cloned.1.call-start = ((), (), s32[]{:S(2)}) async-start(), calls=%async_computation.3 | async-start | bytes 2359296 | tf_op jit(solution)/shard_map/reduce_scatter | solution.py:24
  135.4 1.9 copy-start
  146.3 121.2 %all-gather.5.cloned.1.call-start = ((), (), s32[]{:S(2)}) async-start(), calls=%async_computation.4 | async-start | bytes 2359296 | tf_op jit(solution)/shard_map/all_gather | solution.py:25
  211.7 189.8 %reduce-scatter.5.cloned.1.call-start = ((), (), s32[]{:S(2)}) async-start(), calls=%async_computation.5 | async-start | bytes 8650752 | tf_op jit(solution)/shard_map/reduce_scatter | solution.py:26
Sparse Core Ops, SparseCore 0:
  10.0 107.6 all-gather.2
  146.4 65.2 reduce-scatter.2
  213.5 53.9 all-gather.4
  279.2 122.3 reduce-scatter.4
where the time goes:
time: 408 us
  waiting for transfers between devices  351 us (86%)
  matrix products  29.3 us (7%)
  between operations  13.2 us (3%)
  other arithmetic  7.07 us (2%)
  local copies, waits for them, and re-layouts  6.99 us (2%)
    reduce_scatter x1, waiting for transfers between devices, local(): lax.psum_scatter(lax.dot_general(full, rotation, (((1,), (1,)), ((), ()))...  122 us
    all_gather x1, waiting for transfers between devices, local(): lax.all_gather(stacked, 'tok', axis=1, tiled=True)  108 us
    reduce_scatter x1, waiting for transfers between devices, local(): lax.psum_scatter(mixed_terms, 'hid', scatter_dimension=0, tiled=True)  65.4 us
    all_gather x1, waiting for transfers between devices, local(): full = lax.all_gather(mixed, 'hid', axis=0, tiled=True)  55.7 us
    dot_general x1, matrix products, local(): jnp.einsum('srk,kc->src', lax.all_gather(stacked, 'tok', axis=1, tiled=Tr...  17.7 us
    dot_general x1, matrix products, local(): lax.dot_general(full, rotation, (((1,), (1,)), ((), ())), precision=high,...  11.6 us
  transfers between devices with their start and end apart: 4, of which 4 were waited for; matrix products, arithmetic and copies ran while one was open for 0% of the time, Pallas kernels for 0%

commit v1 on v0

--- a/solution.py
+++ b/solution.py
@@ -11,7 +11,9 @@
     stacked = jnp.stack([base, source])
     terms = jnp.einsum(
         "srk,kc->src",
-        lax.all_gather(stacked, "tok", axis=1, tiled=True),
+        jnp.concatenate(
+            lax.all_to_all(jnp.stack([stacked] * lax.axis_size("tok")), "tok", 0, 0), axis=1
+        ),
         rotation,
         precision=high,
         preferred_element_type=jnp.float32,

time: 408 us -> 672 us (1.65)
  waiting for transfers between devices: 351 us -> 594 us
  local copies, waits for them, and re-layouts: 6.99 us -> 21.9 us
  starting transfers between devices: 0.12 us -> 11.7 us
    all_to_all x0 -> x1, waiting for transfers between devices: none -> 368 us  [local(): lax.all_to_all(jnp.stack([stacked] * lax.axis_size('tok')), 'tok', 0, 0)]
    all_gather x1 -> x0, waiting for transfers between devices: 108 us -> none  [local(): lax.all_gather(stacked, 'tok', axis=1, tiled=True)]
    reduce_scatter x1, waiting for transfers between devices: 65.4 us -> 48.3 us  [local(): lax.psum_scatter(mixed_terms, 'hid', scatter_dimension=0, tiled=True)]
    all_to_all x0 -> x1, starting transfers between devices: none -> 11.6 us  [local(): lax.all_to_all(jnp.stack([stacked] * lax.axis_size('tok')), 'tok', 0, 0)]
    another operation x0 -> x1, local copies, waits for them, and re-layouts: none -> 7.86 us  [local(): jnp.stack([stacked] * lax.axis_size('tok'))]
where the time goes in v1:
time: 672 us
  waiting for transfers between devices  594 us (88%)
  matrix products  26 us (4%)
  local copies, waits for them, and re-layouts  21.9 us (3%)
  between operations  13.2 us (2%)
  starting transfers between devices  11.7 us (2%)
    all_to_all x1, waiting for transfers between devices, local(): lax.all_to_all(jnp.stack([stacked] * lax.axis_size('tok')), 'tok', 0, 0)  368 us
    reduce_scatter x1, waiting for transfers between devices, local(): lax.psum_scatter(lax.dot_general(full, rotation, (((1,), (1,)), ((), ()))...  122 us
    all_gather x1, waiting for transfers between devices, local(): full = lax.all_gather(mixed, 'hid', axis=0, tiled=True)  55.7 us
    reduce_scatter x1, waiting for transfers between devices, local(): lax.psum_scatter(mixed_terms, 'hid', scatter_dimension=0, tiled=True)  48.3 us
    dot_general x1, matrix products, local(): jnp.einsum('srk,kc->src', jnp.concatenate(lax.all_to_all(jnp.stack([stack...  14.4 us
  transfers between devices with their start and end apart: 4, of which 4 were waited for; matrix products, arithmetic and copies ran while one was open for 0% of the time, Pallas kernels for 0%

profile of v1, /device:TPU:8, one launch (start us, length us, event | category | flops | bytes accessed | tf_op | source)
XLA Modules:
  0.0 672.0 jit_solution(14127433460771748661)
XLA Ops:
  6.5 1.1 pad_maximum_fusion
  7.6 7.9 %stack.11 = f32[32,2,32,2048]{3,2,1,0:T(8,128)} broadcast(f32[2,32,2048]{2,1,0:T(8,128)S(1)} %pad_maximum_fusion), dimensions={1,2,3} | broadcast | bytes 17301504 | tf_op jit(solution)/shard_map/stack | solution.py:15
  15.5 0.0 copy-start.2
  15.5 0.0 copy-start.3
  15.5 11.6 %all-to-all-start = ((f32[32,2,32,2048]{3,2,1,0:T(8,128)}), f32[32,2,32,2048]{3,2,1,0:T(8,128)}, u32[]{:S(2)}, u32[]{:S(2)}) async-start(f32[32,2,32,2048]{3,2,1,0:T(8,128)} %stack.11), calls=%async_computation | async-start | bytes 33554432 | tf_op jit(solution)/shard_map/all_to_all | solution.py:15
  27.1 0.0 reduce-scatter.3.cloned.1.call-start
  27.1 0.0 copy-done.2
  27.1 0.0 copy-done.3
  27.2 367.8 %all-to-all-done = f32[32,2,32,2048]{3,2,1,0:T(8,128)} async-done(((f32[32,2,32,2048]{3,2,1,0:T(8,128)}), f32[32,2,32,2048]{3,2,1,0:T(8,128)}, u32[]{:S(2)}, u32[]{:S(2)}) %all-to-all-start) | async-done | bytes 16777248 | tf_op jit(solution)/shard_map/all_to_all | solution.py:15
  395.0 0.0 copy-start.1
  395.0 6.7 copy.6
  401.7 0.3 copy-done.1
  402.0 14.4 %fusion = f32[2,1024,512]{2,1,0:T(8,128)S(1)} fusion(f32[2,1024,2048]{2,1,0:T(8,128)S(1)} %bitcast.16, f32[2048,512]{1,0:T(8,128)S(1)} %copy-done.1), kind=kOutput, calls=%fused_computation.1 | convolution fusion | flops 12884901888 | bytes 25165824 | tf_op jit(solution)/shard_map/srk,kc->src/dot_general | solution.py:12
  416.4 0.0 copy-start
  416.4 1.9 copy-done
  418.4 0.2 slice_bitcast_fusion.1
  418.5 4.9 gather_fusion
  423.4 3.8 fusion.2
  427.2 0.0 reduce-scatter.3.cloned.1.call-update
  427.3 0.0 all-gather.2.cloned.1.call-start
  427.3 48.3 %reduce-scatter.3.cloned.1.call-done = f32[128,512]{1,0:T(8,128)} async-done(((f32[1024,512]{1,0:T(8,128)}), f32[128,512]{1,0:T(8,128)}) %reduce-scatter.3.cloned.1.call-update) | async-done | bytes 262160 | tf_op jit(solution)/shard_map/reduce_scatter | solution.py:26
  475.6 0.0 all-gather.2.cloned.1.call-update
  475.6 0.0 reduce-scatter.5.cloned.1.call-start
  475.7 55.7 %all-gather.2.cloned.1.call-done = f32[1024,512]{1,0:T(8,128)} async-done(((f32[128,512]{1,0:T(8,128)}), f32[1024,512]{1,0:T(8,128)}) %all-gather.2.cloned.1.call-update) | async-done | bytes 2097168 | tf_op jit(solution)/shard_map/all_gather | solution.py:27
  531.4 11.6 %fusion.4 = f32[1024,2048]{1,0:T(8,128)} fusion(f32[1024,512]{1,0:T(8,128)} %all-gather.2.cloned.1.call-done, f32[2048,512]{1,0:T(8,128)} %param.9), kind=kOutput, calls=%fused_computation.11 | convolution fusion | flops 6442450944 | bytes 14680064 | tf_op jit(solution)/shard_map/dot_general | solution.py:29
  543.0 0.0 reduce-scatter.5.cloned.1.call-update
  543.0 122.5 %reduce-scatter.5.cloned.1.call-done = f32[32,2048]{1,0:T(8,128)} async-done(((f32[1024,2048]{1,0:T(8,128)}), f32[32,2048]{1,0:T(8,128)}) %reduce-scatter.5.cloned.1.call-update) | async-done | bytes 262160 | tf_op jit(solution)/shard_map/reduce_scatter | solution.py:28
  (3 shorter events, 0.0 us)
Async XLA Ops:
  15.5 11.7 %copy-start.2 = (s32[1024]{0:T(1024)S(1)}, s32[1024]{0:T(1024)}, u32[]{:S(2)}) copy-start(s32[1024]{0:T(1024)} %param.7) | copy-start | bytes 12292
  15.5 11.7 %copy-start.3 = (s32[1024]{0:T(1024)S(1)}, s32[1024]{0:T(1024)}, u32[]{:S(2)}) copy-start(s32[1024]{0:T(1024)} %param.8) | copy-start | bytes 12292
  15.5 379.5 %all-to-all-start = ((f32[32,2,32,2048]{3,2,1,0:T(8,128)}), f32[32,2,32,2048]{3,2,1,0:T(8,128)}, u32[]{:S(2)}, u32[]{:S(2)}) async-start(f32[32,2,32,2048]{3,2,1,0:T(8,128)} %stack.11), calls=%async_computation | async-start | bytes 33554432 | tf_op jit(solution)/shard_map/all_to_all | solution.py:15
  27.1 448.6 %reduce-scatter.3.cloned.1.call-start = ((), (), s32[]{:S(2)}) async-start(), calls=%async_computation.3 | async-start | bytes 2359296 | tf_op jit(solution)/shard_map/reduce_scatter | solution.py:26
  395.0 7.0 %copy-start.1 = (f32[2048,512]{1,0:T(8,128)S(1)}, f32[2048,512]{1,0:T(8,128)}, u32[]{:S(2)}) copy-start(f32[2048,512]{1,0:T(8,128)} %param.9) | copy-start | bytes 12582916
  416.4 1.9 copy-start
  427.3 104.1 %all-gather.2.cloned.1.call-start = ((), (), s32[]{:S(2)}) async-start(), calls=%async_computation.4 | async-start | bytes 2359296 | tf_op jit(solution)/shard_map/all_gather | solution.py:27
  475.6 189.8 %reduce-scatter.5.cloned.1.call-start = ((), (), s32[]{:S(2)}) async-start(), calls=%async_computation.5 | async-start | bytes 8650752 | tf_op jit(solution)/shard_map/reduce_scatter | solution.py:28
Sparse Core Ops, SparseCore 0:
  427.4 48.1 reduce-scatter.2
  477.4 53.9 all-gather.1
  543.1 122.3 reduce-scatter.4
